TPU v7x, 32 devices: a whole 2x2x4 slice. The times are simulated.
32 devices in a mesh: width: 4 (over z), cb: 4 (over y, x), row: 2 (over core).
Axes of the slice: x: 2, y: 2, z: 4, core: 2. Of those that a mesh axis runs over, the one named last changes fastest.
Arguments:
- weights: bfloat16 [3584, 8192], P(('cb', 'row'), 'width'), as said below
- dir_codes: int32 [3584, 1024], P(('cb', 'row'), 'width'), may hold values from 0 to 65535
- norm_bins: int32 [3584, 1024], P(('cb', 'row'), 'width'), may hold values from 0 to 255, as said below
Outputs:
- codewords: float32 [4096, 128], P('cb')
- norm_levels: float32 [256], replicated
Inputs may be any that keep to these rules, and one draw needn't show every extreme that they name: `weights`: real-valued entries, rows of differing scales. `norm_bins`: the bins of one row all lie in one aligned run of 16 consecutive bins.
All inputs are finite; a program needn't handle non-finite values.
Results may differ from a plain program's by a relative error of at most 0.0003.
Values sent between devices are 32-bit elements; how exact they have to be, the bound alone decides.
A program may use at most 192 MiB of HBM per device.

v0:
```python
import math

import jax
import jax.numpy as jnp
from jax import lax
from jax.sharding import PartitionSpec as P

WIDTH = 8192
CODES = 65536
NBINS = 256


def swapped(array, axis, distance):
    return lax.ppermute(array, axis, [(i, i ^ 1 << distance) for i in range(lax.axis_size(axis))])


def sylvester(matrix_order, out_type):
    indices = jnp.arange(matrix_order, dtype=jnp.int32)
    common = jnp.bitwise_and(indices[:, None], indices[None, :])
    bit_total = jnp.zeros((matrix_order, matrix_order), jnp.int32)
    for bit_place in range(max(matrix_order.bit_length() - 1, 0)):
        bit_total = bit_total + jnp.bitwise_and(jnp.right_shift(common, bit_place), 1)
    parity = bit_total % 2
    return (1 - 2 * parity).astype(out_type)


def bin_totals(log_norms, bin_ids):
    group_count = log_norms.shape[0]
    block_count = 8
    block_size = group_count // block_count
    bin_range = jnp.arange(NBINS, dtype=jnp.int32)

    def accumulate(running, block_item):
        block_logs, block_bins = block_item
        onehot = (block_bins[:, None] == bin_range[None, :]).astype(jnp.float32)
        values = jnp.stack([block_logs, jnp.ones_like(block_logs)], axis=0)
        block_part = jnp.dot(values, onehot, precision=lax.Precision.HIGHEST)
        return (running + block_part, None)

    block_items = (
        log_norms.reshape(block_count, block_size),
        bin_ids.reshape(block_count, block_size),
    )
    running, _ = lax.scan(accumulate, jnp.zeros((2, NBINS), jnp.float32), block_items)
    return (running[0], running[1])


def per_device(weights, dir_codes, norm_bins):
    row_count, col_count = weights.shape
    scaling = 1.0 / math.sqrt(WIDTH)
    width_devices = lax.axis_size("width")
    local_part = jnp.dot(
        weights, sylvester(col_count, jnp.bfloat16), preferred_element_type=jnp.float32
    )
    position = lax.axis_index("width")
    for level_bit in range(width_devices.bit_length() - 1):
        partner = swapped(local_part, "width", level_bit)
        upper_half = position // 2**level_bit % 2 == 1
        local_part = jnp.where(upper_half, partner - local_part, local_part + partner)
    rotated = local_part * scaling
    grouped = rotated.reshape(-1, 8)
    code_flat = dir_codes.reshape(-1)
    bin_flat = norm_bins.reshape(-1)
    group_norms = jnp.sqrt(jnp.sum(grouped * grouped, axis=-1))
    floored = jnp.maximum(group_norms, 1.0)
    directions = grouped / floored[:, None]
    log_norms = jnp.log(floored)
    bin_sums, bin_counts = bin_totals(log_norms, bin_flat)
    total_sums, total_counts = lax.psum((bin_sums, bin_counts), ("width", "cb", "row"))
    norm_levels = total_sums / jnp.maximum(total_counts, 1.0)
    partial_value = jax.ops.segment_sum(directions, code_flat, num_segments=CODES).reshape(-1)
    owned_sums = lax.psum_scatter(partial_value, "cb", scatter_dimension=0, tiled=True)
    code_totals = lax.psum(owned_sums, ("width", "row"))
    summed = code_totals.reshape(-1, 8)
    lengths = jnp.sqrt(jnp.sum(summed * summed, axis=-1))
    codewords = (summed / jnp.maximum(lengths, 1.0)[:, None]).reshape(-1, 128)
    return (codewords, norm_levels)


def solution(mesh):
    return jax.shard_map(
        per_device,
        mesh=mesh,
        in_specs=(P(("cb", "row"), "width"), P(("cb", "row"), "width"), P(("cb", "row"), "width")),
        out_specs=(P("cb", None), P()),
        check_vma=False,
    )
```

profile of v0, /device:TPU:0, one launch (start us, length us, event | category | flops | bytes accessed | tf_op | source)
XLA Modules:
  0.0 1204.9 jit_solution(741284506609880701)
XLA Ops:
  7.3 1.7 copy-done
  8.9 28.6 %fusion.17 = f32[448,2048]{1,0:T(8,128)} fusion(bf16[448,2048]{1,0:T(8,128)(2,1)S(1)} %copy-done), kind=kOutput, calls=%fused_computation.25 | convolution fusion | flops 3955228672 | bytes 5505024 | tf_op jit(solution)/shard_map/dot_general | solution.py:52
  37.5 3.0 collective-permute-start
  40.6 79.6 %collective-permute-done = f32[448,2048]{1,0:T(8,128)} collective-permute-done((f32[448,2048]{1,0:T(8,128)}, f32[448,2048]{1,0:T(8,128)}, u32[]{:S(2)}, u32[]{:S(2)}) %collective-permute-start) | collective-permute-done | bytes 3670048 | tf_op jit(solution)/shard_map/ppermute | solution.py:14
  120.2 6.0 add_select_fusion.1
  126.2 2.8 collective-permute-start.1
  129.1 0.2 copy.11
  129.4 0.6 dynamic-slice
  130.6 156.0 %collective-permute-done.1 = f32[448,2048]{1,0:T(8,128)} collective-permute-done((f32[448,2048]{1,0:T(8,128)}, f32[448,2048]{1,0:T(8,128)}, u32[]{:S(2)}, u32[]{:S(2)}) %collective-permute-start.1) | collective-permute-done | bytes 3670048 | tf_op jit(solution)/shard_map/ppermute | solution.py:14
  286.6 6.1 select_multiply_fusion
  292.7 36.9 %reshape.40 = f32[114688,8]{1,0:T(8,128)} reshape(f32[448,2048]{1,0:T(8,128)} %select_multiply_fusion) | data formatting | bytes 7340032 | tf_op jit(solution)/shard_map/reshape | solution.py:61
  329.6 19.2 %multiply_reduce_fusion = f32[114688]{0:T(1024)S(1)} fusion(f32[114688,8]{1,0:T(8,128)} %reshape.40), kind=kLoop, calls=%fused_computation.12 | loop fusion | flops 1720320 | bytes 4128768 | tf_op jit(solution)/shard_map/reduce_sum | solution.py:64
  349.0 681.3 %scatter_custom_fusion = f32[65536,8]{1,0:T(8,128)} fusion(s32[114688]{0:T(1024)S(1)} %bitcast.17, f32[114688,8]{1,0:T(8,128)} %reshape.40, f32[114688]{0:T(1024)S(1)} %get-tuple-element.60, f32[]{:T(128)} %constant.75.clone.1), kind=kCustom, calls=%fused_computation.10 | custom fusion | flops 1835008 | bytes 6225924 | tf_op jit(solution)/shard_map/scatter-add | solution.py:71
  1030.4 23.7 %reshape.41 = f32[524288]{0:T(1024)} reshape(f32[65536,8]{1,0:T(8,128)} %scatter_custom_fusion) | data formatting | bytes 4194304 | tf_op jit(solution)/shard_map/reshape | solution.py:71
  1054.1 37.0 %while.11 = (s32[]{:T(128)}, f32[2,256]{1,0:T(2,128)S(1)}, f32[8,14336]{1,0:T(8,128)S(1)}, s32[8,14336]{1,0:T(8,128)S(1)}, s32[]{:T(128)}, /*index=5*/s32[]{:T(128)}) while((s32[]{:T(128)}, f32[2,256]{1,0:T(2,128)S(1)}, f32[8,14336]{1,0:T(8,128)S(1)}, s32[8,14336]{1,0:T(8,128)S(1)}, s32[]{:T(128)}, /*index=5*/s32[]{:T(128)}) %tuple.29), condition=%wide.region_6.7_spmd.clone, body=%wide.region_5.6_spmd.clone.sunk | while | flops 91751424 | bytes 348247 | solution.py:44
  1054.2 4.5 fusion.37
  1058.8 4.5 fusion.37
  1063.5 4.5 fusion.37
  1068.1 4.5 fusion.37
  1072.7 4.5 fusion.37
  1077.3 4.5 fusion.37
  1082.0 4.5 fusion.37
  1086.6 4.5 fusion.37
  1091.1 33.7 %all-reduce.8.cloned.1.call-done = f32[524288]{0:T(1024)} async-done(((f32[524288]{0:T(1024)}), f32[524288]{0:T(1024)}) %all-reduce.8.cloned.1.call-update) | async-done | bytes 2097168
  1124.8 1.9 dynamic-slice.1
  1126.7 39.5 %all-reduce.2 = (f32[256]{0:T(256)S(1)}, f32[256]{0:T(256)S(1)}) all-reduce(f32[256]{0:T(256)S(1)} %bitcast.19, f32[256]{0:T(256)S(1)} %bitcast.18), channel_id=1, replica_groups=mesh['width'=4,'cb'=4,'row'=2] {'width','cb','row'}, use_global_device_ids=true, to_apply=%region_7.8 | all-reduce | flops 512 | bytes 4096 | tf_op jit(solution)/shard_map/psum | solution.py:69
  1166.2 0.6 maximum_divide_fusion
  1166.8 17.6 %all-reduce.6.cloned.1.call-done = f32[131072]{0:T(1024)} async-done(((f32[131072]{0:T(1024)}), f32[131072]{0:T(1024)}) %all-reduce.6.cloned.1.call-update) | async-done | bytes 524304 | tf_op jit(solution)/shard_map/psum | solution.py:73
  1184.4 1.3 mul.22
  1185.7 6.1 mul.23
  1191.9 4.6 reduce_sum.19
  1197.2 0.9 bitcast_divide_fusion
  (41 shorter events, 1.8 us)
Async XLA Ops:
  7.2 1.8 copy-start
  7.2 122.2 %copy-start.5 = (u32[32]{0:T(128)S(1)}, u32[32]{0:T(128)}, u32[]{:S(2)}) copy-start(u32[32]{0:T(128)} %constant.95) | copy-start | bytes 388
  7.2 121.8 %copy-start.3 = (s32[448,256]{1,0:T(8,128)S(1)}, s32[448,256]{1,0:T(8,128)}, u32[]{:S(2)}) copy-start(s32[448,256]{1,0:T(8,128)} %param.7) | copy-start | bytes 1376260
  7.2 121.9 %copy-start.4 = (s32[448,256]{1,0:T(8,128)S(1)}, s32[448,256]{1,0:T(8,128)}, u32[]{:S(2)}) copy-start(s32[448,256]{1,0:T(8,128)} %param.6) | copy-start | bytes 1376260
  7.2 1117.6 %all-reduce.8.cloned.1.call-start = ((), (), s32[]{:S(2)}) async-start(), calls=%async_computation.1 | async-start | bytes 4194304
  37.5 82.7 %collective-permute-start = (f32[448,2048]{1,0:T(8,128)}, f32[448,2048]{1,0:T(8,128)}, u32[]{:S(2)}, u32[]{:S(2)}) collective-permute-start(f32[448,2048]{1,0:T(8,128)} %fusion.17), channel_id=1, source_target_pairs={{0,8},{8,0},{16,24},{24,16},{1,9},{9,1},{17,25},{25,17},{2,10},{10... | collective-permute-start | bytes 11010056 | tf_op jit(solution)/shard_map/ppermute | solution.py:14
  126.2 160.4 %collective-permute-start.1 = (f32[448,2048]{1,0:T(8,128)}, f32[448,2048]{1,0:T(8,128)}, u32[]{:S(2)}, u32[]{:S(2)}) collective-permute-start(f32[448,2048]{1,0:T(8,128)} %add_select_fusion.1), channel_id=1, source_target_pairs={{0,16},{8,24},{16,0},{24,8},{1,17},{9,25},{17,1},{25,9},{2,18},{10... | collective-permute-start | bytes 11010056 | tf_op jit(solution)/shard_map/ppermute | solution.py:14
  1054.0 130.4 %all-reduce.6.cloned.1.call-start = ((), (), s32[]{:S(2)}) async-start(), calls=%async_computation | async-start | bytes 1048576 | tf_op jit(solution)/shard_map/psum | solution.py:73
  1091.1 106.9 %copy-start.1 = (bf16[448,2048]{1,0:T(8,128)(2,1)S(1)}, bf16[448,2048]{1,0:T(8,128)(2,1)}, u32[]{:S(2)}) copy-start(bf16[448,2048]{1,0:T(8,128)(2,1)} %param.5) | copy-start | bytes 5505028
  1184.4 12.7 %copy-start.2 = (f32[131072]{0:T(1024)S(1)}, f32[131072]{0:T(1024)}, u32[]{:S(2)}) copy-start(f32[131072]{0:T(1024)} %all-reduce.6.cloned.1.call-done) | copy-start | bytes 1572868
Sparse Core Ops, SparseCore 0:
  1054.2 70.5 all-reduce.7
  1127.8 56.5 all-reduce.5
where the time goes:
time: 1210 us; the launch traced here: 1200 us
  other arithmetic  720 us (60%)
  waiting for transfers between devices  287 us (24%)
  local copies, waits for them, and re-layouts  72.6 us (6%)
  matrix products  64.7 us (5%)
  blocking collectives  39.5 us (3%)
  between operations  14.8 us (1%)
    scatter-add x1, other arithmetic, per_device(): jax.ops.segment_sum(directions, code_flat, num_segments=CODES).reshape(-1)  681 us
    ppermute x2, waiting for transfers between devices, swapped(): lax.ppermute(array, axis, [(i, i ^ 1 << distance) for i in range(lax.axis...  236 us
    psum x1, blocking collectives, per_device(): lax.psum((bin_sums, bin_counts), ('width', 'cb', 'row'))  39.5 us
    reshape x1, local copies, waits for them, and re-layouts, per_device(): grouped = rotated.reshape(-1, 8)  36.9 us
    dot_general x8, matrix products, accumulate(): block_part = jnp.dot(values, onehot, precision=lax.Precision.HIGHEST)  36.1 us
    unnamed x3, waiting for transfers between devices  33.7 us
    dot_general x1, matrix products, per_device(): jnp.dot(weights, sylvester(col_count, jnp.bfloat16), preferred_element_ty...  28.6 us
  transfers between devices with their start and end apart: 4, of which 4 were waited for; matrix products, arithmetic and copies ran while one was open for 3% of the time, Pallas kernels for 0%

commit v1 on v0

v1 whole, which is shorter than its diff:
```python
import functools
import math

import jax
import jax.numpy as jnp
from jax import lax
from jax.experimental import pallas as pl
from jax.experimental.pallas import tpu as pltpu
from jax.sharding import PartitionSpec as P

CODES = 65536
NBINS = 256
VECTOR = 8
RUN = 16
LANES = 256


def parity_sign(x):
    return 1 - 2 * (lax.population_count(x) & 1)


def rotate_kernel(rows, w_ref, y_ref):
    k = pl.program_id(0)
    cols = w_ref.shape[1]
    groups = cols // VECTOR
    i = lax.broadcasted_iota(jnp.int32, (cols, groups), 0)
    j = lax.broadcasted_iota(jnp.int32, (cols, groups), 1) * VECTOR + k
    h = parity_sign(i & j).astype(jnp.float32).astype(jnp.bfloat16)
    out = jnp.dot(w_ref[...], h, preferred_element_type=jnp.float32)
    parts, _, padded, _ = y_ref.shape
    for p in range(parts):
        y_ref[p, 0, :rows, :] = out[p * rows : (p + 1) * rows]
        if padded > rows:
            y_ref[p, 0, rows:, :] = jnp.zeros((padded - rows, groups), jnp.float32)


def rotate(weights, parts):
    total, cols = weights.shape
    rows = total // parts
    padded = -(-rows // 8) * 8
    groups = cols // VECTOR
    return pl.pallas_call(
        functools.partial(rotate_kernel, rows),
        grid=(VECTOR,),
        in_specs=[pl.BlockSpec((total, cols), lambda k: (0, 0))],
        out_specs=pl.BlockSpec((parts, 1, padded, groups), lambda k: (0, k, 0, 0)),
        out_shape=jax.ShapeDtypeStruct((parts, VECTOR, padded, groups), jnp.float32),
        compiler_params=pltpu.CompilerParams(vmem_limit_bytes=48 << 20),
        cost_estimate=pl.CostEstimate(
            flops=2 * total * cols * cols, bytes_accessed=total * cols * 6, transcendentals=0
        ),
        name="rotate",
    )(weights)


def table_kernel(parts, rows, owners, scale, pre_ref, post_ref, *refs):
    y_refs, code_refs, bin_refs = refs[:parts], refs[parts : 2 * parts], refs[2 * parts : 3 * parts]
    table_ref, bins_ref, d_ref, c_ref = refs[3 * parts :]
    step = pl.program_id(0)
    groups = y_refs[0].shape[2]

    @pl.when(step == 0)
    def _():
        table_ref[...] = jnp.zeros_like(table_ref)
        bins_ref[...] = jnp.zeros_like(bins_ref)

    row_ids = lax.broadcasted_iota(jnp.int32, (8, groups), 0) + step * 8
    square = [jnp.zeros((8, groups), jnp.float32) for _ in range(parts)]
    for k in range(VECTOR):
        z = [y_refs[p][k] * pre_ref[p] for p in range(parts)]
        half = 1
        while half < parts:
            z = [z[p ^ half] - z[p] if p & half else z[p] + z[p ^ half] for p in range(parts)]
            half *= 2
        for p in range(parts):
            value = z[p] * (post_ref[p] * scale)
            square[p] = square[p] + value * value
            d_ref[p, k] = value
    run_ids = lax.broadcasted_iota(jnp.int32, (8, NBINS), 1)
    sum_part = jnp.zeros((8, NBINS), jnp.float32)
    count_part = jnp.zeros((8, NBINS), jnp.float32)
    run = bin_refs[0][:, :1] // RUN
    logs, offsets, ones = [], [], []
    for p in range(parts):
        floored = jnp.maximum(jnp.sqrt(square[p]), 1.0)
        inverse = 1.0 / floored
        for k in range(VECTOR):
            d_ref[p, k] = d_ref[p, k] * inverse
        c_ref[p] = code_refs[p][...]
        logs.append(jnp.log(floored))
        offsets.append(bin_refs[p][...] % RUN)
        ones.append((row_ids < rows).astype(jnp.float32))
    for b in range(RUN):
        s = sum(jnp.where(offsets[p] == b, logs[p], 0.0) for p in range(parts))
        n = sum(jnp.where(offsets[p] == b, ones[p], 0.0) for p in range(parts))
        here = run_ids == run * RUN + b
        sum_part = sum_part + jnp.where(here, jnp.sum(s, axis=1, keepdims=True), 0.0)
        count_part = count_part + jnp.where(here, jnp.sum(n, axis=1, keepdims=True), 0.0)
    bins_ref[0] += sum_part
    bins_ref[1] += count_part

    low = CODES // LANES // owners

    def body(index, _):
        p, r = index // 8, index % 8
        code = c_ref[p, pl.ds(r, 1), :]
        u, v = code // LANES, code % LANES
        sub = lax.broadcasted_iota(jnp.int32, (LANES, groups), 0)
        hot_u = (sub == u).astype(jnp.float32).astype(jnp.bfloat16)
        hot_v = (sub == v).astype(jnp.float32).astype(jnp.bfloat16)
        hot_v = jnp.concatenate([hot_v, hot_v], axis=1)
        spread = []
        for k in range(VECTOR):
            d = jnp.broadcast_to(d_ref[p, k, pl.ds(r, 1), :], (16, groups))
            top = d.astype(jnp.bfloat16)
            rest = (d - top.astype(jnp.float32)).astype(jnp.bfloat16)
            spread.append((top, rest))
        blocks = []
        for o in range(owners):
            for k in range(VECTOR):
                for t in range(low // 16):
                    hot = hot_u[o * low + t * 16 : o * low + t * 16 + 16]
                    blocks.append(jnp.concatenate([hot * spread[k][0], hot * spread[k][1]], axis=1))
        left = jnp.concatenate(blocks, axis=0)
        table_ref[...] += lax.dot_general(
            left, hot_v, (((1,), (1,)), ((), ())), preferred_element_type=jnp.float32
        )
        return 0

    lax.fori_loop(0, parts * 8, body, 0)


def table(ys, codes, bins, pre, post, rows, owners):
    parts = len(ys)
    _, padded, groups = ys[0].shape
    scale = 1.0 / math.sqrt(groups * VECTOR * parts)
    height = VECTOR * CODES // LANES
    smem = pl.BlockSpec(memory_space=pltpu.SMEM)
    return pl.pallas_call(
        functools.partial(table_kernel, parts, rows, owners, scale),
        grid=(padded // 8,),
        in_specs=[smem, smem]
        + [pl.BlockSpec((VECTOR, 8, groups), lambda i: (0, i, 0))] * parts
        + [pl.BlockSpec((8, groups), lambda i: (i, 0))] * (2 * parts),
        out_specs=[
            pl.BlockSpec((height, LANES), lambda i: (0, 0)),
            pl.BlockSpec((2, 8, NBINS), lambda i: (0, 0, 0)),
        ],
        out_shape=[
            jax.ShapeDtypeStruct((height, LANES), jnp.float32),
            jax.ShapeDtypeStruct((2, 8, NBINS), jnp.float32),
        ],
        scratch_shapes=[
            pltpu.VMEM((parts, VECTOR, 8, groups), jnp.float32),
            pltpu.VMEM((parts, 8, groups), jnp.int32),
        ],
        compiler_params=pltpu.CompilerParams(vmem_limit_bytes=48 << 20),
        cost_estimate=pl.CostEstimate(
            flops=4 * parts * padded * groups * CODES * VECTOR,
            bytes_accessed=parts * padded * groups * 40,
            transcendentals=0,
        ),
        name="direction_table",
    )(pre, post, *ys, *codes, *bins)


def exchanged(array, axis, parts, me):
    def block(d):
        return lax.dynamic_index_in_dim(array, me ^ d, 0, keepdims=False)

    return [block(0)] + [
        lax.ppermute(block(d), axis, [(i, i ^ d) for i in range(parts)]) for d in range(1, parts)
    ]


def per_device(weights, dir_codes, norm_bins):
    parts, owners = lax.axis_size("width"), lax.axis_size("cb")
    me = lax.axis_index("width")
    rows = weights.shape[0] // parts
    padded = -(-rows // 8) * 8

    def split(ids):
        ids = ids.reshape(parts, rows, -1)
        return jnp.pad(ids, ((0, 0), (0, padded - rows), (0, 0)))

    codes = exchanged(split(dir_codes), "width", parts, me)
    bins = exchanged(split(norm_bins), "width", parts, me)
    ys = exchanged(rotate(weights, parts), "width", parts, me)
    others = jnp.arange(parts, dtype=jnp.int32)
    pre = parity_sign(others & me).astype(jnp.float32)
    post = parity_sign((others ^ me) & me).astype(jnp.float32)
    sums, bin_part = table(ys, codes, bins, pre, post, rows, owners)
    bin_part = lax.psum(jnp.sum(bin_part, axis=1), ("width", "cb", "row"))
    norm_levels = bin_part[0] / jnp.maximum(bin_part[1], 1.0)
    owned = lax.psum_scatter(sums.reshape(-1, 128), "cb", scatter_dimension=0, tiled=True)
    owned = lax.psum(owned, ("width", "row")).reshape(VECTOR, -1)
    lengths = jnp.sqrt(jnp.sum(owned * owned, axis=0))
    words = owned / jnp.maximum(lengths, 1.0)[None]
    return (words.T.reshape(-1, 128), norm_levels)


def solution(mesh):
    spec = P(("cb", "row"), "width")
    return jax.shard_map(
        per_device,
        mesh=mesh,
        in_specs=(spec, spec, spec),
        out_specs=(P("cb", None), P()),
        check_vma=False,
    )
```

time: 1210 us -> 591 us (0.49)
  other arithmetic: 720 us -> 2.96 us
  Pallas kernels: 0 us -> 353 us
  waiting for transfers between devices: 287 us -> 119 us
  matrix products: 64.7 us -> 0 us
  local copies, waits for them, and re-layouts: 72.6 us -> 22.6 us
  starting transfers between devices: 5.88 us -> 39.8 us
    scatter-add x1 -> x0, other arithmetic: 681 us -> none  [per_device(): jax.ops.segment_sum(directions, code_flat, num_segments=CODES).reshape(-1)]
    pallas_call x0 -> x2, Pallas kernels: none -> 353 us  [the longest x1 347 us: table(): pl.pallas_call(functools.partial(table_kernel, parts, rows, owners, scale...]
    ppermute x2 -> x9, waiting for transfers between devices: 236 us -> 66.8 us  [exchanged(): lax.ppermute(block(d), axis, [(i, i ^ d) for i in range(parts)])]
    dot_general x9 -> x0, matrix products: 64.7 us -> none  [the longest x8 36.1 us: accumulate(): block_part = jnp.dot(values, onehot, precision=lax.Precision.HIGHEST)]
    reshape x2 -> x3, local copies, waits for them, and re-layouts: 60.5 us -> 11.6 us  [the longest x1 7.07 us: per_device(): return (words.T.reshape(-1, 128), norm_levels)]
    reduce_scatter x0 -> x1, waiting for transfers between devices: none -> 34.4 us  [per_device(): lax.psum_scatter(sums.reshape(-1, 128), 'cb', scatter_dimension=0, tiled=...]
    ppermute x2 -> x9, starting transfers between devices: 5.8 us -> 39.7 us  [exchanged(): lax.ppermute(block(d), axis, [(i, i ^ d) for i in range(parts)])]
    unnamed x3 -> x2, waiting for transfers between devices: 33.7 us -> 0.03 us
  transfers between devices with their start and end apart: 4 -> 11, of which waited for: 4 -> 7; matrix products, arithmetic and copies ran while one was open for 3% -> 0% of each run, Pallas kernels for 0% -> 0%
where the time goes in v1:
time: 591 us
  Pallas kernels  353 us (60%)
  waiting for transfers between devices  119 us (20%)
  starting transfers between devices  39.8 us (7%)
  blocking collectives  39.4 us (7%)
  local copies, waits for them, and re-layouts  22.6 us (4%)
  between operations  14.1 us (2%)
    pallas_call x1, Pallas kernels, table(): pl.pallas_call(functools.partial(table_kernel, parts, rows, owners, scale...  347 us
    ppermute x9, waiting for transfers between devices, exchanged(): lax.ppermute(block(d), axis, [(i, i ^ d) for i in range(parts)])  66.8 us
    ppermute x9, starting transfers between devices, exchanged(): lax.ppermute(block(d), axis, [(i, i ^ d) for i in range(parts)])  39.7 us
    psum x1, blocking collectives, per_device(): bin_part = lax.psum(jnp.sum(bin_part, axis=1), ('width', 'cb', 'row'))  39.4 us
    reduce_scatter x1, waiting for transfers between devices, per_device(): lax.psum_scatter(sums.reshape(-1, 128), 'cb', scatter_dimension=0, tiled=...  34.4 us
    psum x1, waiting for transfers between devices, per_device(): owned = lax.psum(owned, ('width', 'row')).reshape(VECTOR, -1)  17.7 us
  transfers between devices with their start and end apart: 11, of which 7 were waited for; matrix products, arithmetic and copies ran while one was open for 0% of the time, Pallas kernels for 0%

profile of v1, /device:TPU:0, one launch (start us, length us, event | category | flops | bytes accessed | tf_op | source)
XLA Modules:
  0.0 590.9 jit_solution(16501518210314261854)
XLA Ops:
  7.2 0.0 reduce-scatter.2.cloned.1.call-start
  7.2 1.5 copy-done.1
  8.7 6.4 %rotate.1 = f32[4,8,112,256]{3,2,1,0:T(8,128)S(1)} custom-call(bf16[448,2048]{1,0:T(8,128)(2,1)S(1)} %copy-done.1), custom_call_target="tpu_custom_call" | custom-call | flops 3758096384 | bytes 5505024 | tf_op jit(solution)/shard_map/rotate/pallas_call | solution.py:42
  15.1 1.8 copy-done
  16.9 2.3 dynamic-slice_bitcast_fusion
  19.2 5.1 collective-permute-start.2
  24.3 0.0 collective-permute-start.1
  24.4 0.6 collective-permute-start
  25.0 3.8 collective-permute-start.5
  28.9 58.6 %collective-permute-done.5.refs_7_ = s32[112,256]{1,0:T(8,128)S(1)} collective-permute-done((s32[112,256]{1,0:T(8,128)S(1)}, s32[112,256]{1,0:T(8,128)S(1)}, u32[]{:S(2)}, u32[]{:S(2)}) %collective-permute-start.5) | collective-permute-done | bytes 114720 | tf_op jit(solution)/shard_map/ppermute | solution.py:172
  87.5 24.2 %collective-permute-start.3 = (s32[112,256]{1,0:T(8,128)S(1)}, s32[112,256]{1,0:T(8,128)S(1)}, u32[]{:S(2)}, u32[]{:S(2)}) collective-permute-start(s32[112,256]{1,0:T(8,128)S(1)} %get-tuple-element.16), channel_id=1, source_target_pairs={{0,8},{8,0},{16,24},{24,16},{1,9},{9,1},{17,25},{25,17},{2,10},{10... | collective-permute-start | bytes 344072 | tf_op jit(solution)/shard_map/ppermute | solution.py:172
  111.7 1.0 collective-permute-done.4.refs_6_
  112.8 2.7 collective-permute-start.8
  115.5 0.0 collective-permute-done.3.refs_5_
  115.5 3.2 collective-permute-start.7
  118.7 2.1 collective-permute-done.8.refs_11_
  120.8 3.6 collective-permute-done.7.refs_10_
  124.4 1.4 collective-permute-done.6.refs_9_
  125.8 346.8 %direction_table.1 = (f32[2048,256]{1,0:T(8,128)}, f32[2,8,256]{2,1,0:T(8,128)S(1)}) custom-call(f32[4]{0:T(128)S(1)} %get-tuple-element.19.pre_ref, f32[4]{0:T(128)S(1)} %get-tuple-element.18.post_ref, f32[8,112,256]{2,1,0:T(8,128)S(1)} %get-tuple-element.9.refs_0_, f32[8,112,256]{2,1,0:T(8,128)S(1)} %collective-permute-done.refs_1_, ...), custom_call_target="tpu_custom_call" | custom-call | flops 240518168576 | bytes 4587520 | tf_op jit(solution)/shard_map/direction_table/pallas_call | solution.py:139
  472.6 2.6 reshape.28
  475.3 0.0 reduce-scatter.2.cloned.1.call-update
  475.3 0.0 all-reduce.2.cloned.1.call-start
  475.3 34.4 %reduce-scatter.2.cloned.1.call-done = f32[1024,128]{1,0:T(8,128)} async-done(((f32[4096,128]{1,0:T(8,128)}), f32[1024,128]{1,0:T(8,128)}) %reduce-scatter.2.cloned.1.call-update) | async-done | bytes 524304 | tf_op jit(solution)/shard_map/reduce_scatter | solution.py:195
  509.7 1.9 reshape.29
  511.7 0.0 all-reduce.2.cloned.1.call-update
  511.7 39.4 %psum.15 = f32[2,256]{1,0:T(2,128)S(1)} all-reduce(f32[2,256]{1,0:T(2,128)S(1)} %reduce_sum.19), channel_id=1, replica_groups=mesh['width'=4,'cb'=4,'row'=2] {'width','cb','row'}, use_global_device_ids=true, to_apply=%region_4.5 | all-reduce | flops 512 | bytes 4096 | tf_op jit(solution)/shard_map/psum | solution.py:193
  551.1 0.6 fusion
  551.7 17.7 %all-reduce.2.cloned.1.call-done = f32[8,16384]{1,0:T(8,128)} async-done(((f32[8,16384]{1,0:T(8,128)}), f32[8,16384]{1,0:T(8,128)}) %all-reduce.2.cloned.1.call-update) | async-done | bytes 524304 | tf_op jit(solution)/shard_map/psum | solution.py:196
  569.3 1.2 multiply_reduce_fusion
  570.6 1.1 divide_bitcast_fusion
  571.7 5.3 copy.6
  577.0 7.1 %reshape.30 = f32[1024,128]{1,0:T(8,128)} reshape(f32[16384,8]{1,0:T(8,128)} %copy.6) | data formatting | bytes 1048576 | tf_op jit(solution)/shard_map/reshape | solution.py:199
  (16 shorter events, 0.1 us)
Async XLA Ops:
  7.2 502.6 %reduce-scatter.2.cloned.1.call-start = ((), (), s32[]{:S(2)}) async-start(), calls=%async_computation.1 | async-start | bytes 2621440 | tf_op jit(solution)/shard_map/reduce_scatter | solution.py:195
  7.2 1.5 copy-start.1
  15.1 1.8 copy-start
  16.9 8.1 %copy-start.2 = (s32[448,256]{1,0:T(8,128)S(1)}, s32[448,256]{1,0:T(8,128)}, u32[]{:S(2)}) copy-start(s32[448,256]{1,0:T(8,128)} %param.4) | copy-start | bytes 1376260
  16.9 11.9 %copy-start.3 = (s32[448,256]{1,0:T(8,128)S(1)}, s32[448,256]{1,0:T(8,128)}, u32[]{:S(2)}) copy-start(s32[448,256]{1,0:T(8,128)} %param.5) | copy-start | bytes 1376260
  19.2 106.6 %collective-permute-start.2 = (f32[8,112,256]{2,1,0:T(8,128)S(1)}, f32[8,112,256]{2,1,0:T(8,128)S(1)}, u32[]{:S(2)}, u32[]{:S(2)}) collective-permute-start(f32[8,112,256]{2,1,0:T(8,128)S(1)} %get-tuple-element.6), channel_id=1, source_target_pairs={{0,24},{8,16},{16,8},{24,0},{1,25},{9,17},{17,9},{25,1},{2,26},{10... | collective-permute-start | bytes 2752520 | tf_op jit(solution)/shard_map/ppermute | solution.py:172
  24.3 101.5 %collective-permute-start.1 = (f32[8,112,256]{2,1,0:T(8,128)S(1)}, f32[8,112,256]{2,1,0:T(8,128)S(1)}, u32[]{:S(2)}, u32[]{:S(2)}) collective-permute-start(f32[8,112,256]{2,1,0:T(8,128)S(1)} %get-tuple-element.7), channel_id=1, source_target_pairs={{0,16},{8,24},{16,0},{24,8},{1,17},{9,25},{17,1},{25,9},{2,18},{10... | collective-permute-start | bytes 2752520 | tf_op jit(solution)/shard_map/ppermute | solution.py:172
  24.4 101.5 %collective-permute-start = (f32[8,112,256]{2,1,0:T(8,128)S(1)}, f32[8,112,256]{2,1,0:T(8,128)S(1)}, u32[]{:S(2)}, u32[]{:S(2)}) collective-permute-start(f32[8,112,256]{2,1,0:T(8,128)S(1)} %get-tuple-element.8), channel_id=1, source_target_pairs={{0,8},{8,0},{16,24},{24,16},{1,9},{9,1},{17,25},{25,17},{2,10},{10... | collective-permute-start | bytes 2752520 | tf_op jit(solution)/shard_map/ppermute | solution.py:172
  25.0 62.5 %collective-permute-start.5 = (s32[112,256]{1,0:T(8,128)S(1)}, s32[112,256]{1,0:T(8,128)S(1)}, u32[]{:S(2)}, u32[]{:S(2)}) collective-permute-start(s32[112,256]{1,0:T(8,128)S(1)} %get-tuple-element.14), channel_id=1, source_target_pairs={{0,24},{8,16},{16,8},{24,0},{1,25},{9,17},{17,9},{25,1},{2,26},{10... | collective-permute-start | bytes 344072 | tf_op jit(solution)/shard_map/ppermute | solution.py:172
  28.8 83.9 %collective-permute-start.4 = (s32[112,256]{1,0:T(8,128)S(1)}, s32[112,256]{1,0:T(8,128)S(1)}, u32[]{:S(2)}, u32[]{:S(2)}) collective-permute-start(s32[112,256]{1,0:T(8,128)S(1)} %get-tuple-element.15), channel_id=1, source_target_pairs={{0,16},{8,24},{16,0},{24,8},{1,17},{9,25},{17,1},{25,9},{2,18},{10... | collective-permute-start | bytes 344072 | tf_op jit(solution)/shard_map/ppermute | solution.py:172
  87.5 28.0 %collective-permute-start.3 = (s32[112,256]{1,0:T(8,128)S(1)}, s32[112,256]{1,0:T(8,128)S(1)}, u32[]{:S(2)}, u32[]{:S(2)}) collective-permute-start(s32[112,256]{1,0:T(8,128)S(1)} %get-tuple-element.16), channel_id=1, source_target_pairs={{0,8},{8,0},{16,24},{24,16},{1,9},{9,1},{17,25},{25,17},{2,10},{10... | collective-permute-start | bytes 344072 | tf_op jit(solution)/shard_map/ppermute | solution.py:172
  112.8 8.0 %collective-permute-start.8 = (s32[112,256]{1,0:T(8,128)S(1)}, s32[112,256]{1,0:T(8,128)S(1)}, u32[]{:S(2)}, u32[]{:S(2)}) collective-permute-start(s32[112,256]{1,0:T(8,128)S(1)} %get-tuple-element.10), channel_id=1, source_target_pairs={{0,24},{8,16},{16,8},{24,0},{1,25},{9,17},{17,9},{25,1},{2,26},{10... | collective-permute-start | bytes 344072 | tf_op jit(solution)/shard_map/ppermute | solution.py:172
  115.5 8.9 %collective-permute-start.7 = (s32[112,256]{1,0:T(8,128)S(1)}, s32[112,256]{1,0:T(8,128)S(1)}, u32[]{:S(2)}, u32[]{:S(2)}) collective-permute-start(s32[112,256]{1,0:T(8,128)S(1)} %get-tuple-element.11), channel_id=1, source_target_pairs={{0,16},{8,24},{16,0},{24,8},{1,17},{9,25},{17,1},{25,9},{2,18},{10... | collective-permute-start | bytes 344072 | tf_op jit(solution)/shard_map/ppermute | solution.py:172
  120.8 5.1 collective-permute-start.6
  475.3 94.1 %all-reduce.2.cloned.1.call-start = ((), (), s32[]{:S(2)}) async-start(), calls=%async_computation.2 | async-start | bytes 1048576 | tf_op jit(solution)/shard_map/psum | solution.py:196
Sparse Core Ops, SparseCore 0:
  475.4 34.2 reduce-scatter.1
  512.7 56.5 all-reduce.1

commit v2 on v1

--- a/solution.py
+++ b/solution.py
@@ -13,6 +13,7 @@
 VECTOR = 8
 RUN = 16
 LANES = 256
+JOIN = 2
 
 
 def parity_sign(x):
@@ -53,18 +54,18 @@
     )(weights)
 
 
-def table_kernel(parts, rows, owners, scale, pre_ref, post_ref, *refs):
+def table_kernel(parts, rows, first, owners, scale, pre_ref, post_ref, *refs):
     y_refs, code_refs, bin_refs = refs[:parts], refs[parts : 2 * parts], refs[2 * parts : 3 * parts]
-    table_ref, bins_ref, d_ref, c_ref = refs[3 * parts :]
+    *before, table_ref, bins_ref, d_ref, c_ref = refs[3 * parts :]
     step = pl.program_id(0)
     groups = y_refs[0].shape[2]
 
     @pl.when(step == 0)
     def _():
-        table_ref[...] = jnp.zeros_like(table_ref)
-        bins_ref[...] = jnp.zeros_like(bins_ref)
-
-    row_ids = lax.broadcasted_iota(jnp.int32, (8, groups), 0) + step * 8
+        table_ref[...] = before[0][...] if before else jnp.zeros_like(table_ref)
+        bins_ref[...] = before[1][...] if before else jnp.zeros_like(bins_ref)
+
+    row_ids = lax.broadcasted_iota(jnp.int32, (8, groups), 0) + (step * 8 + first)
     square = [jnp.zeros((8, groups), jnp.float32) for _ in range(parts)]
     for k in range(VECTOR):
         z = [y_refs[p][k] * pre_ref[p] for p in range(parts)]
@@ -102,50 +103,55 @@
     low = CODES // LANES // owners
 
     def body(index, _):
-        p, r = index // 8, index % 8
-        code = c_ref[p, pl.ds(r, 1), :]
-        u, v = code // LANES, code % LANES
-        sub = lax.broadcasted_iota(jnp.int32, (LANES, groups), 0)
-        hot_u = (sub == u).astype(jnp.float32).astype(jnp.bfloat16)
-        hot_v = (sub == v).astype(jnp.float32).astype(jnp.bfloat16)
-        hot_v = jnp.concatenate([hot_v, hot_v], axis=1)
-        spread = []
-        for k in range(VECTOR):
-            d = jnp.broadcast_to(d_ref[p, k, pl.ds(r, 1), :], (16, groups))
-            top = d.astype(jnp.bfloat16)
-            rest = (d - top.astype(jnp.float32)).astype(jnp.bfloat16)
-            spread.append((top, rest))
-        blocks = []
-        for o in range(owners):
+        p, r = index // 8 * JOIN, index % 8
+        lefts, rights = [], []
+        for q in range(JOIN):
+            code = c_ref[p + q, pl.ds(r, 1), :]
+            u, v = code // LANES, code % LANES
+            sub = lax.broadcasted_iota(jnp.int32, (LANES, groups), 0)
+            hot_u = (sub == u).astype(jnp.float32).astype(jnp.bfloat16)
+            hot_v = (sub == v).astype(jnp.float32).astype(jnp.bfloat16)
+            rights += [hot_v, hot_v]
+            tops, rests = [], []
+            spread = []
             for k in range(VECTOR):
-                for t in range(low // 16):
-                    hot = hot_u[o * low + t * 16 : o * low + t * 16 + 16]
-                    blocks.append(jnp.concatenate([hot * spread[k][0], hot * spread[k][1]], axis=1))
-        left = jnp.concatenate(blocks, axis=0)
+                d = jnp.broadcast_to(d_ref[p + q, k, pl.ds(r, 1), :], (16, groups))
+                top = d.astype(jnp.bfloat16)
+                spread.append((top, (d - top.astype(jnp.float32)).astype(jnp.bfloat16)))
+            for o in range(owners):
+                for k in range(VECTOR):
+                    for t in range(low // 16):
+                        hot = hot_u[o * low + t * 16 : o * low + t * 16 + 16]
+                        tops.append(hot * spread[k][0])
+                        rests.append(hot * spread[k][1])
+            lefts += [jnp.concatenate(tops, axis=0), jnp.concatenate(rests, axis=0)]
         table_ref[...] += lax.dot_general(
-            left, hot_v, (((1,), (1,)), ((), ())), preferred_element_type=jnp.float32
+            jnp.concatenate(lefts, axis=1),
+            jnp.concatenate(rights, axis=1),
+            (((1,), (1,)), ((), ())),
+            preferred_element_type=jnp.float32,
         )
         return 0
 
-    lax.fori_loop(0, parts * 8, body, 0)
-
-
-def table(ys, codes, bins, pre, post, rows, owners):
+    lax.fori_loop(0, parts // JOIN * 8, body, 0)
+
+
+def table(ys, codes, bins, pre, post, rows, first, owners, before):
     parts = len(ys)
     _, padded, groups = ys[0].shape
     scale = 1.0 / math.sqrt(groups * VECTOR * parts)
     height = VECTOR * CODES // LANES
     smem = pl.BlockSpec(memory_space=pltpu.SMEM)
+    sums_spec = pl.BlockSpec((height, LANES), lambda i: (0, 0))
+    bins_spec = pl.BlockSpec((2, 8, NBINS), lambda i: (0, 0, 0))
     return pl.pallas_call(
-        functools.partial(table_kernel, parts, rows, owners, scale),
+        functools.partial(table_kernel, parts, rows, first, owners, scale),
         grid=(padded // 8,),
         in_specs=[smem, smem]
         + [pl.BlockSpec((VECTOR, 8, groups), lambda i: (0, i, 0))] * parts
-        + [pl.BlockSpec((8, groups), lambda i: (i, 0))] * (2 * parts),
-        out_specs=[
-            pl.BlockSpec((height, LANES), lambda i: (0, 0)),
-            pl.BlockSpec((2, 8, NBINS), lambda i: (0, 0, 0)),
-        ],
+        + [pl.BlockSpec((8, groups), lambda i: (i, 0))] * (2 * parts)
+        + [sums_spec, bins_spec][: len(before)],
+        out_specs=[sums_spec, bins_spec],
         out_shape=[
             jax.ShapeDtypeStruct((height, LANES), jnp.float32),
             jax.ShapeDtypeStruct((2, 8, NBINS), jnp.float32),
@@ -161,7 +167,143 @@
             transcendentals=0,
         ),
         name="direction_table",
-    )(pre, post, *ys, *codes, *bins)
+    )(pre, post, *ys, *codes, *bins, *before)
+
+
+def reduce_kernel(phases, owners, low, t_ref, b_ref, words_ref, levels_ref, *scratch):
+    count = len(phases)
+    recvs, held = scratch[:count], scratch[count : 2 * count]
+    bin_recv, bin_held, send, recv, bin_send, bin_got, gather_send, gather_got = scratch[2 * count :]
+    places = {axis: lax.axis_index(axis) for axis, _ in phases}
+    partners = [{axis: places[axis] ^ bit} for axis, bit in phases]
+    barrier = pltpu.get_barrier_semaphore()
+    for partner in partners:
+        pl.semaphore_signal(barrier, inc=1, device_id=partner, device_id_type=pl.DeviceIdType.MESH)
+    pl.semaphore_wait(barrier, count)
+
+    bin_held[0] = jnp.sum(b_ref[...], axis=1)
+    now, many, height, offset = t_ref, owners, low, 0
+    gathers = []
+    for n, (axis, bit) in enumerate(phases):
+        mine = places[axis] // bit % 2
+        if axis == "cb":
+            many //= 2
+            source = now.at[pl.ds((1 - mine) * many, many)]
+            kept = now.at[pl.ds(mine * many, many)]
+        elif height > 8:
+            height //= 2
+            source = now.at[:, :, pl.ds(pl.multiple_of((1 - mine) * height, 8), height)]
+            kept = now.at[:, :, pl.ds(pl.multiple_of(mine * height, 8), height)]
+            offset = offset + mine * height
+            gathers.append((n, height, offset))
+        else:
+            source, kept = now, now
+        main = pltpu.make_async_remote_copy(
+            src_ref=source,
+            dst_ref=recvs[n],
+            send_sem=send.at[n],
+            recv_sem=recv.at[n],
+            device_id=partners[n],
+            device_id_type=pl.DeviceIdType.MESH,
+        )
+        side = pltpu.make_async_remote_copy(
+            src_ref=bin_held.at[n],
+            dst_ref=bin_recv.at[n],
+            send_sem=bin_send.at[n],
+            recv_sem=bin_got.at[n],
+            device_id=partners[n],
+            device_id_type=pl.DeviceIdType.MESH,
+        )
+        main.start()
+        side.start()
+        side.wait()
+        bin_held[n + 1] = bin_held[n] + bin_recv[n]
+        main.wait()
+        held[n][...] = kept[...] + recvs[n][...]
+        now = held[n]
+
+    totals = bin_held[count]
+    levels_ref[...] = totals[:1] / jnp.maximum(totals[1:], 1.0)
+
+    values = [now[0, k] for k in range(VECTOR)]
+    lengths = jnp.sqrt(sum(value * value for value in values))
+    inverse = 1.0 / jnp.maximum(lengths, 1.0)
+    across = 128 // VECTOR
+    down = LANES // across
+    line = lax.broadcasted_iota(jnp.int32, (down, LANES), 0)
+    spot = lax.broadcasted_iota(jnp.int32, (down, LANES), 1)
+    chosen = spot // across == line
+    source = lax.broadcasted_iota(jnp.int32, (LANES, 128), 0)
+    target = lax.broadcasted_iota(jnp.int32, (LANES, 128), 1)
+    total = jnp.zeros((height * down, 128), jnp.float32)
+    for k in range(VECTOR):
+        value = values[k] * inverse
+        spread = jnp.concatenate(
+            [
+                jnp.where(chosen, jnp.broadcast_to(value[i : i + 1], (down, LANES)), 0.0)
+                for i in range(height)
+            ],
+            axis=0,
+        )
+        select = (target == source % across * VECTOR + k).astype(jnp.float32).astype(jnp.bfloat16)
+        for _ in range(3):
+            part = spread.astype(jnp.bfloat16)
+            total = total + jnp.dot(part, select, preferred_element_type=jnp.float32)
+            spread = spread - part.astype(jnp.float32)
+    words_ref[pl.ds(pl.multiple_of(offset * down, 8), height * down), :] = total
+
+    for n, size, start in reversed(gathers):
+        region = words_ref.at[pl.ds(pl.multiple_of(start * down, 8), size * down)]
+        copy = pltpu.make_async_remote_copy(
+            src_ref=region,
+            dst_ref=region,
+            send_sem=gather_send.at[n],
+            recv_sem=gather_got.at[n],
+            device_id=partners[n],
+            device_id_type=pl.DeviceIdType.MESH,
+        )
+        copy.start()
+        copy.wait()
+
+
+def reduced(sums, bin_part, parts, owners, cores):
+    low = CODES // LANES // owners
+
+    def bits(axis, size):
+        return [(axis, 1 << n) for n in range(size.bit_length() - 1)]
+
+    phases = bits("row", cores) + bits("cb", owners)[::-1] + bits("width", parts)
+    count = len(phases)
+    buffers = []
+    many, height = owners, low
+    for axis, _ in phases:
+        if axis == "cb":
+            many //= 2
+        elif height > 8:
+            height //= 2
+        buffers.append(pltpu.VMEM((many, VECTOR, height, LANES), jnp.float32))
+    vmem = pl.BlockSpec(memory_space=pltpu.VMEM)
+    dma = pltpu.SemaphoreType.DMA((count,))
+    return pl.pallas_call(
+        functools.partial(reduce_kernel, phases, owners, low),
+        in_specs=[vmem, vmem],
+        out_specs=[vmem, vmem],
+        out_shape=[
+            jax.ShapeDtypeStruct((CODES * VECTOR // owners // 128, 128), jnp.float32),
+            jax.ShapeDtypeStruct((1, NBINS), jnp.float32),
+        ],
+        scratch_shapes=buffers
+        + buffers
+        + [
+            pltpu.VMEM((count, 2, NBINS), jnp.float32),
+            pltpu.VMEM((count + 1, 2, NBINS), jnp.float32),
+        ]
+        + [dma] * 6,
+        compiler_params=pltpu.CompilerParams(
+            collective_id=0, has_side_effects=True, vmem_limit_bytes=32 << 20
+        ),
+        name="reduce_words",
+    )(sums.reshape(owners, VECTOR, low, LANES), bin_part)
 
 
 def exchanged(array, axis, parts, me):
@@ -174,7 +316,7 @@
 
 
 def per_device(weights, dir_codes, norm_bins):
-    parts, owners = lax.axis_size("width"), lax.axis_size("cb")
+    parts, owners, cores = (lax.axis_size(axis) for axis in ("width", "cb", "row"))
     me = lax.axis_index("width")
     rows = weights.shape[0] // parts
     padded = -(-rows // 8) * 8
@@ -183,20 +325,23 @@
         ids = ids.reshape(parts, rows, -1)
         return jnp.pad(ids, ((0, 0), (0, padded - rows), (0, 0)))
 
-    codes = exchanged(split(dir_codes), "width", parts, me)
-    bins = exchanged(split(norm_bins), "width", parts, me)
-    ys = exchanged(rotate(weights, parts), "width", parts, me)
     others = jnp.arange(parts, dtype=jnp.int32)
     pre = parity_sign(others & me).astype(jnp.float32)
     post = parity_sign((others ^ me) & me).astype(jnp.float32)
-    sums, bin_part = table(ys, codes, bins, pre, post, rows, owners)
-    bin_part = lax.psum(jnp.sum(bin_part, axis=1), ("width", "cb", "row"))
-    norm_levels = bin_part[0] / jnp.maximum(bin_part[1], 1.0)
-    owned = lax.psum_scatter(sums.reshape(-1, 128), "cb", scatter_dimension=0, tiled=True)
-    owned = lax.psum(owned, ("width", "row")).reshape(VECTOR, -1)
-    lengths = jnp.sqrt(jnp.sum(owned * owned, axis=0))
-    words = owned / jnp.maximum(lengths, 1.0)[None]
-    return (words.T.reshape(-1, 128), norm_levels)
+    codes, bins, turned = split(dir_codes), split(norm_bins), rotate(weights, parts)
+    edge = max(padded // 8 // 4, 1) * 8
+    chunks = [(0, edge), (edge, padded)]
+    arrived = []
+    for start, stop in chunks:
+        sent = (turned[:, :, start:stop], codes[:, start:stop], bins[:, start:stop])
+        if arrived:
+            sent, arrived[-1] = lax.optimization_barrier((sent, arrived[-1]))
+        arrived.append([exchanged(array, "width", parts, me) for array in sent])
+    before = []
+    for (start, _), (ys, ids, runs) in zip(chunks, arrived):
+        before = table(ys, ids, runs, pre, post, rows, start, owners, before)
+    codewords, norm_levels = reduced(*before, parts, owners, cores)
+    return (codewords, norm_levels.reshape(-1))
 
 
 def solution(mesh):

time: 591 us -> 425 us (0.72)
  waiting for transfers between devices: 119 us -> 27.2 us
  blocking collectives: 39.4 us -> 0 us
  local copies, waits for them, and re-layouts: 22.6 us -> 6.58 us
  between operations: 14.1 us -> 0.85 us
  starting transfers between devices: 39.8 us -> 30.1 us
  Pallas kernels: 353 us -> 360 us
    ppermute x9 -> x18, waiting for transfers between devices: 66.8 us -> 27.2 us  [exchanged(): lax.ppermute(block(d), axis, [(i, i ^ d) for i in range(parts)])]
    psum x1 -> x0, blocking collectives: 39.4 us -> none  [per_device(): bin_part = lax.psum(jnp.sum(bin_part, axis=1), ('width', 'cb', 'row'))]
    reduce_scatter x1 -> x0, waiting for transfers between devices: 34.4 us -> none  [per_device(): lax.psum_scatter(sums.reshape(-1, 128), 'cb', scatter_dimension=0, tiled=...]
    psum x1 -> x0, waiting for transfers between devices: 17.7 us -> none  [per_device(): owned = lax.psum(owned, ('width', 'row')).reshape(VECTOR, -1)]
    reshape x3 -> x0, local copies, waits for them, and re-layouts: 11.6 us -> none  [the longest x1 7.07 us: per_device(): return (words.T.reshape(-1, 128), norm_levels)]
    ppermute x9 -> x18, starting transfers between devices: 39.7 us -> 30.1 us  [exchanged(): lax.ppermute(block(d), axis, [(i, i ^ d) for i in range(parts)])]
    pallas_call x1 -> x3, Pallas kernels: 347 us -> 354 us  [the longest x2 310 us: table(): pl.pallas_call(functools.partial(table_kernel, parts, rows, first, owners...]
  transfers between devices with their start and end apart: 11 -> 18, of which waited for: 7 -> 7; matrix products, arithmetic and copies ran while one was open for 0% -> 0% of each run, Pallas kernels for 0% -> 16%
where the time goes in v2:
time: 425 us
  Pallas kernels  360 us (85%)
  starting transfers between devices  30.1 us (7%)
  waiting for transfers between devices  27.2 us (6%)
  local copies, waits for them, and re-layouts  6.58 us (2%)
    pallas_call x2, Pallas kernels, table(): pl.pallas_call(functools.partial(table_kernel, parts, rows, first, owners...  310 us
    pallas_call x1, Pallas kernels, reduced(): pl.pallas_call(functools.partial(reduce_kernel, phases, owners, low), in_...  43.5 us
    ppermute x18, starting transfers between devices, exchanged(): lax.ppermute(block(d), axis, [(i, i ^ d) for i in range(parts)])  30.1 us
    ppermute x18, waiting for transfers between devices, exchanged(): lax.ppermute(block(d), axis, [(i, i ^ d) for i in range(parts)])  27.2 us
  transfers between devices with their start and end apart: 18, of which 7 were waited for; matrix products, arithmetic and copies ran while one was open for 0% of the time, Pallas kernels for 16%

profile of v2, /device:TPU:0, one launch (start us, length us, event | category | flops | bytes accessed | tf_op | source)
XLA Modules:
  0.0 425.2 jit_solution(12841554310602983627)
XLA Ops:
  0.7 1.5 copy-done.1
  2.1 6.4 %rotate.1 = f32[4,8,112,256]{3,2,1,0:T(8,128)S(1)} custom-call(bf16[448,2048]{1,0:T(8,128)(2,1)S(1)} %copy-done.1), custom_call_target="tpu_custom_call" | custom-call | flops 3758096384 | bytes 5505024 | tf_op jit(solution)/shard_map/rotate/pallas_call | solution.py:43
  8.5 1.8 copy-done
  10.4 0.1 dynamic-slice_bitcast_fusion.4
  10.5 3.1 collective-permute-start
  13.6 2.6 collective-permute-start.1
  16.2 1.0 collective-permute-start.3
  17.2 3.5 collective-permute-start.4
  20.7 6.3 %collective-permute-done.3.refs_5_ = s32[24,256]{1,0:T(8,128)S(1)} collective-permute-done((s32[24,256]{1,0:T(8,128)S(1)}, s32[24,256]{1,0:T(8,128)S(1)}, u32[]{:S(2)}, u32[]{:S(2)}) %collective-permute-start.3) | collective-permute-done | bytes 24608 | tf_op jit(solution)/shard_map/ppermute | solution.py:314
  27.0 2.5 collective-permute-start.5
  29.5 5.9 %collective-permute-done.4.refs_6_ = s32[24,256]{1,0:T(8,128)S(1)} collective-permute-done((s32[24,256]{1,0:T(8,128)S(1)}, s32[24,256]{1,0:T(8,128)S(1)}, u32[]{:S(2)}, u32[]{:S(2)}) %collective-permute-start.4) | collective-permute-done | bytes 24608 | tf_op jit(solution)/shard_map/ppermute | solution.py:314
  35.4 3.0 collective-permute-start.7
  38.4 0.8 collective-permute-done.6.refs_9_
  39.2 2.5 collective-permute-start.8
  41.7 3.2 collective-permute-done.8.refs_11_
  45.1 3.0 collective-permute-start.13
  48.1 1.4 collective-permute-start.14
  49.6 0.3 dynamic-slice_bitcast_fusion
  49.9 2.1 collective-permute-start.9
  52.0 0.7 collective-permute-done.12.refs_5_
  52.7 0.3 collective-permute-start.10
  53.0 2.0 collective-permute-start.11
  55.0 0.4 collective-permute-done.14.refs_7_
  55.4 1.6 collective-permute-start.16
  57.1 9.9 %collective-permute-done.15.refs_9_ = s32[88,256]{1,0:T(8,128)S(1)} collective-permute-done((s32[88,256]{1,0:T(8,128)S(1)}, s32[88,256]{1,0:T(8,128)S(1)}, u32[]{:S(2)}, u32[]{:S(2)}) %collective-permute-start.15) | collective-permute-done | bytes 90144 | tf_op jit(solution)/shard_map/ppermute | solution.py:314
  67.0 1.4 collective-permute-start.17
  68.4 66.7 %direction_table.2 = (f32[2048,256]{1,0:T(8,128)S(1)}, f32[2,8,256]{2,1,0:T(8,128)S(1)}) custom-call(f32[4]{0:T(128)S(1)} %get-tuple-element.69.pre_ref, f32[4]{0:T(128)S(1)} %get-tuple-element.68.post_ref, f32[8,24,256]{2,1,0:T(8,128)S(1)} %get-tuple-element.26.refs_0_, f32[8,24,256]{2,1,0:T(8,128)S(1)} %collective-permute-done.refs_1_, ...), custom_call_target="tpu_custom_call" | custom-call | flops 51539607552 | bytes 983040 | tf_op jit(solution)/shard_map/direction_table/pallas_call | solution.py:147
  135.1 1.3 copy-done.2
  136.5 243.8 %direction_table.3 = (f32[2048,256]{1,0:T(8,128)S(1)}, f32[2,8,256]{2,1,0:T(8,128)S(1)}) custom-call(f32[4]{0:T(128)S(1)} %get-tuple-element.69.pre_ref, f32[4]{0:T(128)S(1)} %get-tuple-element.68.post_ref, f32[8,88,256]{2,1,0:T(8,128)S(1)} %get-tuple-element.47.refs_0_, f32[8,88,256]{2,1,0:T(8,128)S(1)} %collective-permute-done.9.refs_1_, ...), custom_call_target="tpu_custom_call" | custom-call | flops 188978561024 | bytes 3604480 | tf_op jit(solution)/shard_map/direction_table/pallas_call | solution.py:147
  380.3 43.5 %reduce_words.1 = (f32[1024,128]{1,0:T(8,128)S(1)}, f32[1,256]{1,0:T(1,128)S(1)}) custom-call(f32[4,8,64,256]{3,2,1,0:T(8,128)S(1)} %bitcast.52, f32[2,8,256]{2,1,0:T(8,128)S(1)} %get-tuple-element.41.b_ref), custom_call_target="tpu_custom_call" | custom-call | tf_op jit(solution)/shard_map/reduce_words/pallas_call | solution.py:287
  423.8 0.8 copy.7
  424.6 0.6 copy.8
  (34 shorter events, 0.4 us)
Async XLA Ops:
  0.6 1.5 copy-start.1
  8.5 1.8 copy-start
  10.3 5.9 %copy-start.3 = (s32[448,256]{1,0:T(8,128)S(1)}, s32[448,256]{1,0:T(8,128)}, u32[]{:S(2)}) copy-start(s32[448,256]{1,0:T(8,128)} %param.4) | copy-start | bytes 1376260
  10.3 10.3 %copy-start.4 = (s32[448,256]{1,0:T(8,128)S(1)}, s32[448,256]{1,0:T(8,128)}, u32[]{:S(2)}) copy-start(s32[448,256]{1,0:T(8,128)} %param.5) | copy-start | bytes 1376260
  10.5 34.5 %collective-permute-start = (f32[8,24,256]{2,1,0:T(8,128)S(1)}, f32[8,24,256]{2,1,0:T(8,128)S(1)}, u32[]{:S(2)}, u32[]{:S(2)}) collective-permute-start(f32[8,24,256]{2,1,0:T(8,128)S(1)} %get-tuple-element.50), channel_id=1, source_target_pairs={{0,8},{8,0},{16,24},{24,16},{1,9},{9,1},{17,25},{25,17},{2,10},{10... | collective-permute-start | bytes 589832 | tf_op jit(solution)/shard_map/ppermute | solution.py:314
  13.6 31.4 %collective-permute-start.1 = (f32[8,24,256]{2,1,0:T(8,128)S(1)}, f32[8,24,256]{2,1,0:T(8,128)S(1)}, u32[]{:S(2)}, u32[]{:S(2)}) collective-permute-start(f32[8,24,256]{2,1,0:T(8,128)S(1)} %get-tuple-element.49), channel_id=1, source_target_pairs={{0,16},{8,24},{16,0},{24,8},{1,17},{9,25},{17,1},{25,9},{2,18},{10... | collective-permute-start | bytes 589832 | tf_op jit(solution)/shard_map/ppermute | solution.py:314
  16.1 28.8 %collective-permute-start.2 = (f32[8,24,256]{2,1,0:T(8,128)S(1)}, f32[8,24,256]{2,1,0:T(8,128)S(1)}, u32[]{:S(2)}, u32[]{:S(2)}) collective-permute-start(f32[8,24,256]{2,1,0:T(8,128)S(1)} %get-tuple-element.48), channel_id=1, source_target_pairs={{0,24},{8,16},{16,8},{24,0},{1,25},{9,17},{17,9},{25,1},{2,26},{10... | collective-permute-start | bytes 589832 | tf_op jit(solution)/shard_map/ppermute | solution.py:314
  16.2 10.8 %collective-permute-start.3 = (s32[24,256]{1,0:T(8,128)S(1)}, s32[24,256]{1,0:T(8,128)S(1)}, u32[]{:S(2)}, u32[]{:S(2)}) collective-permute-start(s32[24,256]{1,0:T(8,128)S(1)} %get-tuple-element.66), channel_id=1, source_target_pairs={{0,8},{8,0},{16,24},{24,16},{1,9},{9,1},{17,25},{25,17},{2,10},{10... | collective-permute-start | bytes 73736 | tf_op jit(solution)/shard_map/ppermute | solution.py:314
  17.2 18.2 %collective-permute-start.4 = (s32[24,256]{1,0:T(8,128)S(1)}, s32[24,256]{1,0:T(8,128)S(1)}, u32[]{:S(2)}, u32[]{:S(2)}) collective-permute-start(s32[24,256]{1,0:T(8,128)S(1)} %get-tuple-element.65), channel_id=1, source_target_pairs={{0,16},{8,24},{16,0},{24,8},{1,17},{9,25},{17,1},{25,9},{2,18},{10... | collective-permute-start | bytes 73736 | tf_op jit(solution)/shard_map/ppermute | solution.py:314
  27.0 8.4 %collective-permute-start.5 = (s32[24,256]{1,0:T(8,128)S(1)}, s32[24,256]{1,0:T(8,128)S(1)}, u32[]{:S(2)}, u32[]{:S(2)}) collective-permute-start(s32[24,256]{1,0:T(8,128)S(1)} %get-tuple-element.64), channel_id=1, source_target_pairs={{0,24},{8,16},{16,8},{24,0},{1,25},{9,17},{17,9},{25,1},{2,26},{10... | collective-permute-start | bytes 73736 | tf_op jit(solution)/shard_map/ppermute | solution.py:314
  35.3 3.8 collective-permute-start.6
  35.4 6.4 %collective-permute-start.7 = (s32[24,256]{1,0:T(8,128)S(1)}, s32[24,256]{1,0:T(8,128)S(1)}, u32[]{:S(2)}, u32[]{:S(2)}) collective-permute-start(s32[24,256]{1,0:T(8,128)S(1)} %get-tuple-element.61), channel_id=1, source_target_pairs={{0,16},{8,24},{16,0},{24,8},{1,17},{9,25},{17,1},{25,9},{2,18},{10... | collective-permute-start | bytes 73736 | tf_op jit(solution)/shard_map/ppermute | solution.py:314
  39.2 5.8 %collective-permute-start.8 = (s32[24,256]{1,0:T(8,128)S(1)}, s32[24,256]{1,0:T(8,128)S(1)}, u32[]{:S(2)}, u32[]{:S(2)}) collective-permute-start(s32[24,256]{1,0:T(8,128)S(1)} %get-tuple-element.60), channel_id=1, source_target_pairs={{0,24},{8,16},{16,8},{24,0},{1,25},{9,17},{17,9},{25,1},{2,26},{10... | collective-permute-start | bytes 73736 | tf_op jit(solution)/shard_map/ppermute | solution.py:314
  41.7 7.9 %slice-start = ((f32[4,8,112,256]{3,2,1,0:T(8,128)}), f32[4,8,88,256]{3,2,1,0:T(8,128)S(1)}, s32[]{:S(2)}) async-start(f32[4,8,112,256]{3,2,1,0:T(8,128)} %copy-done), calls=%async_computation | async-start | bytes 5767168 | tf_op jit(solution)/shard_map/slice | solution.py:336
  45.0 7.7 %collective-permute-start.12 = (s32[88,256]{1,0:T(8,128)S(1)}, s32[88,256]{1,0:T(8,128)S(1)}, u32[]{:S(2)}, u32[]{:S(2)}) collective-permute-start(s32[88,256]{1,0:T(8,128)S(1)} %get-tuple-element.58), channel_id=1, source_target_pairs={{0,8},{8,0},{16,24},{24,16},{1,9},{9,1},{17,25},{25,17},{2,10},{10... | collective-permute-start | bytes 270344 | tf_op jit(solution)/shard_map/ppermute | solution.py:314
  45.1 7.9 %collective-permute-start.13 = (s32[88,256]{1,0:T(8,128)S(1)}, s32[88,256]{1,0:T(8,128)S(1)}, u32[]{:S(2)}, u32[]{:S(2)}) collective-permute-start(s32[88,256]{1,0:T(8,128)S(1)} %get-tuple-element.57), channel_id=1, source_target_pairs={{0,16},{8,24},{16,0},{24,8},{1,17},{9,25},{17,1},{25,9},{2,18},{10... | collective-permute-start | bytes 270344 | tf_op jit(solution)/shard_map/ppermute | solution.py:314
  48.1 7.4 %collective-permute-start.14 = (s32[88,256]{1,0:T(8,128)S(1)}, s32[88,256]{1,0:T(8,128)S(1)}, u32[]{:S(2)}, u32[]{:S(2)}) collective-permute-start(s32[88,256]{1,0:T(8,128)S(1)} %get-tuple-element.56), channel_id=1, source_target_pairs={{0,24},{8,16},{16,8},{24,0},{1,25},{9,17},{17,9},{25,1},{2,26},{10... | collective-permute-start | bytes 270344 | tf_op jit(solution)/shard_map/ppermute | solution.py:314
  49.5 17.5 %collective-permute-start.15 = (s32[88,256]{1,0:T(8,128)S(1)}, s32[88,256]{1,0:T(8,128)S(1)}, u32[]{:S(2)}, u32[]{:S(2)}) collective-permute-start(s32[88,256]{1,0:T(8,128)S(1)} %get-tuple-element.54), channel_id=1, source_target_pairs={{0,8},{8,0},{16,24},{24,16},{1,9},{9,1},{17,25},{25,17},{2,10},{10... | collective-permute-start | bytes 270344 | tf_op jit(solution)/shard_map/ppermute | solution.py:314
  49.9 86.5 %collective-permute-start.9 = (f32[8,88,256]{2,1,0:T(8,128)S(1)}, f32[8,88,256]{2,1,0:T(8,128)S(1)}, u32[]{:S(2)}, u32[]{:S(2)}) collective-permute-start(f32[8,88,256]{2,1,0:T(8,128)S(1)} %get-tuple-element.46), channel_id=1, source_target_pairs={{0,8},{8,0},{16,24},{24,16},{1,9},{9,1},{17,25},{25,17},{2,10},{10... | collective-permute-start | bytes 2162696 | tf_op jit(solution)/shard_map/ppermute | solution.py:314
  52.7 83.7 %collective-permute-start.10 = (f32[8,88,256]{2,1,0:T(8,128)S(1)}, f32[8,88,256]{2,1,0:T(8,128)S(1)}, u32[]{:S(2)}, u32[]{:S(2)}) collective-permute-start(f32[8,88,256]{2,1,0:T(8,128)S(1)} %get-tuple-element.45), channel_id=1, source_target_pairs={{0,16},{8,24},{16,0},{24,8},{1,17},{9,25},{17,1},{25,9},{2,18},{10... | collective-permute-start | bytes 2162696 | tf_op jit(solution)/shard_map/ppermute | solution.py:314
  53.0 83.4 %collective-permute-start.11 = (f32[8,88,256]{2,1,0:T(8,128)S(1)}, f32[8,88,256]{2,1,0:T(8,128)S(1)}, u32[]{:S(2)}, u32[]{:S(2)}) collective-permute-start(f32[8,88,256]{2,1,0:T(8,128)S(1)} %get-tuple-element.44), channel_id=1, source_target_pairs={{0,24},{8,16},{16,8},{24,0},{1,25},{9,17},{17,9},{25,1},{2,26},{10... | collective-permute-start | bytes 2162696 | tf_op jit(solution)/shard_map/ppermute | solution.py:314
  55.4 81.0 %collective-permute-start.16 = (s32[88,256]{1,0:T(8,128)S(1)}, s32[88,256]{1,0:T(8,128)S(1)}, u32[]{:S(2)}, u32[]{:S(2)}) collective-permute-start(s32[88,256]{1,0:T(8,128)S(1)} %get-tuple-element.53), channel_id=1, source_target_pairs={{0,16},{8,24},{16,0},{24,8},{1,17},{9,25},{17,1},{25,9},{2,18},{10... | collective-permute-start | bytes 270344 | tf_op jit(solution)/shard_map/ppermute | solution.py:314
  67.0 69.4 %collective-permute-start.17 = (s32[88,256]{1,0:T(8,128)S(1)}, s32[88,256]{1,0:T(8,128)S(1)}, u32[]{:S(2)}, u32[]{:S(2)}) collective-permute-start(s32[88,256]{1,0:T(8,128)S(1)} %get-tuple-element.52), channel_id=1, source_target_pairs={{0,24},{8,16},{16,8},{24,0},{1,25},{9,17},{17,9},{25,1},{2,26},{10... | collective-permute-start | bytes 270344 | tf_op jit(solution)/shard_map/ppermute | solution.py:314
  135.1 1.4 copy-start.2
